TPU v7x, 32 devices: a whole 2x2x4 slice. The times are simulated.
32 devices in a mesh: groups: 2 (over x), adapter: 16 (over z, y, core).
Axes of the slice: x: 2, y: 2, z: 4, core: 2. Of those that a mesh axis runs over, the one named last changes fastest.
Arguments:
- queries: bfloat16 [512, 4096], P(('groups', 'adapter')), parts along dimension 0, may hold values from -4.5 to 4.5
- key_cache: bfloat16 [512, 160, 512], P(('groups', 'adapter')), parts along dimension 0, may hold values from -4.5 to 4.5
- value_cache: bfloat16 [512, 160, 512], P(('groups', 'adapter')), parts along dimension 0, may hold values from -4.5 to 4.5
- lengths: int32 [512], P(('groups', 'adapter')), parts along dimension 0, may hold values from 2 to 160, as said below
- adapter_ids: int32 [512], P(('groups', 'adapter')), parts along dimension 0, may hold values from 0 to 511, as said below
- output_weight_rows: bfloat16 [4096, 8192], P(None, 'adapter'), may hold values from -0.09375 to 0.09375
- basis_in: bfloat16 [4096, 256], replicated, may hold values from -0.09375 to 0.09375
- shared_output_basis: bfloat16 [8192, 256], P('adapter'), may hold values from -0.375 to 0.375
- coefficients: bfloat16 [512, 256, 256], P('adapter'), may hold values from -0.375 to 0.375
Outputs:
- output: bfloat16 [512, 8192], P('groups', 'adapter'), parts along dimension 0
There are 2 independent parts, one for each index of `groups`. A program takes and returns all parts, laid end to end along the dimension named above; an argument that names none is the same for every part. Nothing has to cross between parts.
Inputs may be any that keep to these rules, and one draw needn't show every extreme that they name: `lengths`: every request has at least two positions in use; in every group some request has exactly 160. `adapter_ids`: within a group at most 32 requests have ids in one block of ids b * 32 to (b + 1) * 32 - 1, and some block has exactly 32.
All inputs are finite; a program needn't handle non-finite values.
Results may differ from a plain program's by a relative error of at most 0.014.
Values may be sent and summed in bfloat16 or wider, within the bound.
A program may use at most 64 MiB of HBM per device.

v0:
```python
import jax
import jax.numpy as jnp
from jax import lax
from jax.sharding import PartitionSpec as P

HEAD_DIM = 128
Q_HEADS = 32
KV_HEADS = 4
CTX = 160
CAP = 32


def attend(queries, key_cache, value_cache, lengths):
    req_count = queries.shape[0]
    group_size = Q_HEADS // KV_HEADS
    query_rows = queries.reshape(req_count, KV_HEADS, group_size, HEAD_DIM)
    key_rows = key_cache.reshape(req_count, CTX, KV_HEADS, HEAD_DIM)
    value_rows = value_cache.reshape(req_count, CTX, KV_HEADS, HEAD_DIM)
    scores = jnp.einsum(
        "rkgd,rtkd->rkgt", query_rows, key_rows, preferred_element_type=jnp.float32
    ) * HEAD_DIM ** (-0.5)
    valid_mask = (jnp.arange(CTX, dtype=jnp.int32)[None, :] < lengths[:, None])[:, None, None, :]
    scores = jnp.where(valid_mask, scores, -1e30)
    row_max = jnp.max(scores, axis=-1, keepdims=True)
    exp_terms = jnp.where(valid_mask, jnp.exp(scores - row_max), 0.0)
    prob_weights = (exp_terms / jnp.sum(exp_terms, axis=-1, keepdims=True)).astype(jnp.bfloat16)
    attended = jnp.einsum(
        "rkgt,rtkd->rkgd", prob_weights, value_rows, preferred_element_type=jnp.float32
    )
    return attended.reshape(req_count, Q_HEADS * HEAD_DIM).astype(jnp.bfloat16)


def on_device(
    queries,
    key_cache,
    value_cache,
    lengths,
    adapter_ids,
    output_weight_rows,
    basis_in,
    shared_output_basis,
    coefficients,
):
    attended = attend(queries, key_cache, value_cache, lengths)
    owners = lax.axis_size("adapter")
    my_index = lax.axis_index("adapter")
    projected = jnp.dot(attended, basis_in, preferred_element_type=jnp.float32).astype(jnp.bfloat16)
    all_projected, every_adapter_index = (
        lax.all_gather(projected, "adapter", axis=0, tiled=True),
        lax.all_gather(adapter_ids, "adapter", axis=0, tiled=True),
    )
    base_contribution = jnp.dot(
        lax.all_gather(attended, "adapter", axis=0, tiled=True),
        output_weight_rows,
        preferred_element_type=jnp.float32,
    )
    per_owner = coefficients.shape[0]
    owner_of = every_adapter_index // per_owner
    owner_list = jnp.arange(owners, dtype=jnp.int32)
    owner_match_count = (owner_of[:, None] == owner_list[None, :]).astype(jnp.int32)
    earlier = jnp.cumsum(owner_match_count, axis=0) - owner_match_count
    slot_of = jnp.sum(earlier * owner_match_count, axis=1)
    slot_list = jnp.arange(CAP, dtype=jnp.int32)
    picks = (owner_of[None, :] == my_index) & (slot_of[None, :] == slot_list[:, None])
    pick_matrix = picks.astype(jnp.bfloat16)
    local_ids = jnp.sum(
        jnp.where(picks, every_adapter_index[None, :] % per_owner, 0), axis=1
    ).astype(jnp.int32)
    bucket_rows = jnp.dot(pick_matrix, all_projected, preferred_element_type=jnp.float32).astype(
        jnp.bfloat16
    )
    chosen_coef = coefficients[local_ids]
    bucket_out = jnp.einsum(
        "sk,skj->sj", bucket_rows, chosen_coef, preferred_element_type=jnp.float32
    ).astype(jnp.bfloat16)
    placed = jnp.einsum("sr,sj->rj", pick_matrix, bucket_out, preferred_element_type=jnp.float32)
    adapter_applied = lax.psum(placed, "adapter").astype(jnp.bfloat16)
    low_rank_contribution = lax.dot_general(
        adapter_applied,
        shared_output_basis,
        (((1,), (1,)), ((), ())),
        preferred_element_type=jnp.float32,
    )
    return (base_contribution + low_rank_contribution).astype(jnp.bfloat16)


def solution(mesh):
    return jax.shard_map(
        on_device,
        mesh=mesh,
        in_specs=(
            P(("groups", "adapter"), None),
            P(("groups", "adapter"), None, None),
            P(("groups", "adapter"), None, None),
            P(("groups", "adapter")),
            P(("groups", "adapter")),
            P(None, "adapter"),
            P(),
            P("adapter", None),
            P("adapter", None, None),
        ),
        out_specs=P("groups", "adapter"),
        check_vma=False,
    )
```

profile of v0, /device:TPU:0, one launch (start us, length us, event | category | flops | bytes accessed | tf_op | source)
XLA Modules:
  0.0 131.4 jit_solution(6790126163469824104)
XLA Ops:
  6.5 0.0 copy-start
  6.5 0.0 all-gather.2.cloned.1.call-start
  6.5 1.1 copy.23
  7.6 0.7 iota_compare_fusion.3
  8.3 0.0 copy-done
  8.4 1.6 %fusion.38 = (f32[16,4,8]{2,1,0:T(4,128)S(1)}, f32[16,4,8,160]{3,2,1,0:T(8,128)S(1)}) fusion(pred[16,160]{1,0:T(8,128)(4,1)S(1)} %iota_compare_fusion.3, bf16[16,4,8,128]{3,2,1,0:T(8,128)(2,1)S(1)} %bitcast.74, bf16[16,160,512]{2,1,0:T(8,128)(2,1)S(1)} %copy-done), kind=kOutput, calls=%fused_computation.55 | convolution fusion | flops 21381280 | bytes 3084800 | tf_op jit(solution)/shard_map/sub | solution.py:25
  10.0 0.0 copy-start.3
  10.0 0.0 copy-start.2
  10.0 2.6 %fusion.17 = bf16[16,4,8,128]{3,2,1,0:T(8,128)(2,1)S(1)} fusion(f32[16,4,8,160]{3,2,1,0:T(8,128)S(1)} %get-tuple-element.8, f32[16,4,8]{2,1,0:T(4,128)S(1)} %get-tuple-element.7, bf16[16,160,512]{2,1,0:T(8,128)(2,1)} %param.11), kind=kOutput, calls=%fused_computation.15 | convolution fusion | flops 21200896 | bytes 3082240 | tf_op jit(solution)/shard_map/rkgt,rtkd->rkgd/dot_general | solution.py:27
  12.6 0.7 copy.48
  13.3 0.0 all-gather.2.cloned.1.call-update
  13.4 0.0 copy-done.3
  13.4 0.7 dynamic-slice
  14.7 0.0 copy-done.2
  14.7 0.2 dynamic-update-slice
  15.0 13.7 %all-reduce = s32[256]{0:T(256)S(1)} all-reduce(s32[256]{0:T(256)S(1)} %dynamic-update-slice), channel_id=1, replica_groups=mesh['groups'=2,'adapter'=16] {'adapter'}, use_global_device_ids=true, to_apply=%add | all-reduce | flops 256 | bytes 2048
  28.7 0.6 reduce-window.6
  29.3 0.2 slice_reduce_fusion
  29.6 0.1 fusion.31
  29.7 0.1 select_reduce_fusion
  29.8 4.9 %gather_fusion = bf16[32,256,256]{2,1,0:T(8,128)(2,1)} fusion(bf16[32,256,256]{2,1,0:T(8,128)(2,1)} %param.17, s32[1024]{0:T(1024)S(1)} %pad_clamp_fusion), kind=kCustom, calls=%fused_computation | custom fusion | bytes 8388736 | tf_op jit(solution)/shard_map/gather | solution.py:72
  34.7 2.0 %convolution_convert_fusion.1 = bf16[16,256]{1,0:T(8,128)(2,1)S(1)} fusion(bf16[4096,256]{1,0:T(8,128)(2,1)} %param.15, bf16[2,8,32,128]{3,2,1,0:T(8,128)(2,1)S(1)} %bitcast.71), kind=kOutput, calls=%fused_computation.18 | convolution fusion | flops 33558528 | bytes 2236416 | tf_op jit(solution)/shard_map/dot_general | solution.py:47
  36.7 18.5 %all_gather.11 = bf16[256,256]{1,0:T(8,128)(2,1)S(1)} all-gather(bf16[16,256]{1,0:T(8,128)(2,1)S(1)} %convolution_convert_fusion.1), channel_id=1, replica_groups=mesh['groups'=2,'adapter'=16] {'adapter'}, dimensions={0}, use_global_device_ids=true | all-gather | bytes 139264 | tf_op jit(solution)/shard_map/all_gather | solution.py:49
  55.2 0.1 fusion.20
  55.3 2.9 %fusion.23 = bf16[32,1,256]{2,1,0:T(2,128)(2,1)S(1)} fusion(bf16[32,256,256]{2,1,0:T(8,128)(2,1)} %gather_fusion, bf16[32,256,1]{1,0,2:T(8,128)(2,1)S(1)} %fusion.20), kind=kOutput, calls=%fused_computation.24 | convolution fusion | flops 4194304 | bytes 4227072 | tf_op jit(solution)/shard_map/sk,skj->sj/dot_general | solution.py:73
  58.2 0.2 fusion.26
  58.5 61.0 %all-reduce.2 = bf16[256,256]{1,0:T(8,128)(2,1)S(1)} all-reduce(f32[256,256]{1,0:T(8,128)S(1)} %fusion.26), channel_id=1, replica_groups=mesh['groups'=2,'adapter'=16] {'adapter'}, use_global_device_ids=true, to_apply=%region_6.7 | all-reduce | flops 65536 | bytes 393216 | tf_op jit(solution)/shard_map/psum | solution.py:77
  119.5 0.0 copy-start.1
  119.5 0.0 all-gather.2.cloned.1.call-done
  119.5 4.1 %fusion.41 = f32[256,512]{1,0:T(8,128)S(1)} fusion(bf16[256,4096]{1,0:T(8,128)(2,1)} %all-gather.2.cloned.1.call-done, bf16[4096,512]{1,0:T(8,128)(2,1)} %param.14), kind=kOutput, calls=%fused_computation.56 | convolution fusion | flops 1073741824 | bytes 6815744 | tf_op jit(solution)/shard_map/dot_general | solution.py:52
  123.6 0.0 copy-done.1
  123.6 1.0 fusion.16
  (8 shorter events, 0.1 us)
Async XLA Ops:
  6.5 1.8 %copy-start = (bf16[16,160,512]{2,1,0:T(8,128)(2,1)S(1)}, bf16[16,160,512]{2,1,0:T(8,128)(2,1)}, u32[]{:S(2)}) copy-start(bf16[16,160,512]{2,1,0:T(8,128)(2,1)} %param.10) | copy-start | bytes 7864324
  6.5 113.0 %all-gather.2.cloned.1.call-start = ((), (), s32[]{:S(2)}) async-start(), calls=%async_computation | async-start | bytes 2228224 | tf_op jit(solution)/shard_map/all_gather | solution.py:53
  10.0 3.4 %copy-start.3 = (u32[32]{0:T(128)S(1)}, u32[32]{0:T(128)}, u32[]{:S(2)}) copy-start(u32[32]{0:T(128)} %constant.54) | copy-start | bytes 388
  10.0 4.7 %copy-start.2 = (s32[16]{0:T(128)S(1)}, s32[16]{0:T(128)}, u32[]{:S(2)}) copy-start(s32[16]{0:T(128)} %param.13) | copy-start | bytes 196
  119.5 4.1 %copy-start.1 = (bf16[512,256]{1,0:T(8,128)(2,1)S(1)}, bf16[512,256]{1,0:T(8,128)(2,1)}, u32[]{:S(2)}) copy-start(bf16[512,256]{1,0:T(8,128)(2,1)} %param.16) | copy-start | bytes 786436
Sparse Core Ops, SparseCore 0:
  13.5 44.3 all-gather.1
where the time goes:
time: 132 us; the launch traced here: 131 us
  blocking collectives  93.2 us (71%)
  matrix products  14.5 us (11%)
  between operations  14.2 us (11%)
  local copies, waits for them, and re-layouts  7.84 us (6%)
  other arithmetic  1.61 us (1%)
    psum x1, blocking collectives, on_device(): adapter_applied = lax.psum(placed, 'adapter').astype(jnp.bfloat16)  61 us
    all_gather x1, blocking collectives, on_device(): lax.all_gather(projected, 'adapter', axis=0, tiled=True)  18.5 us
    unnamed x1, blocking collectives  13.7 us
    gather x1, local copies, waits for them, and re-layouts, on_device(): chosen_coef = coefficients[local_ids]  4.93 us
    dot_general x1, matrix products, on_device(): jnp.dot(lax.all_gather(attended, 'adapter', axis=0, tiled=True), output_w...  4.09 us
    dot_general x1, matrix products, on_device(): jnp.einsum('sk,skj->sj', bucket_rows, chosen_coef, preferred_element_type...  2.89 us
    unnamed x13, local copies, waits for them, and re-layouts  2.72 us
  transfers between devices with their start and end apart: 1, of which 0 were waited for; matrix products, arithmetic and copies ran while one was open for 9% of the time, Pallas kernels for 0%

commit v1 on v0

v1 whole, which is shorter than its diff:
```python
import functools

import jax
import jax.numpy as jnp
from jax import lax
from jax.experimental import pallas as pl
from jax.experimental.pallas import tpu as pltpu
from jax.sharding import PartitionSpec as P

HEAD_DIM = 128
Q_HEADS = 32
KV_HEADS = 4
CAP = 32
PAIRS = KV_HEADS // 2
GROUP = Q_HEADS // KV_HEADS
F32 = jnp.float32
BF16 = jnp.bfloat16


def kernel(
    zs,
    ys,
    lengths,
    ids,
    q_hbm,
    k_hbm,
    v_hbm,
    w_hbm,
    basis_hbm,
    sob_hbm,
    coef_hbm,
    out_ref,
    q_buf,
    k_buf,
    v_buf,
    w_buf,
    basis_buf,
    sob_buf,
    coef_buf,
    q32,
    a32,
    att_all,
    proj_all,
    res_all,
    acc,
    local_sem,
    send_sem,
    recv_sem,
):
    n = zs * ys * 2
    me = lax.axis_index("adapter")
    core = lax.rem(me, 2)
    y = lax.rem(lax.div(me, 2), ys)
    z = lax.div(me, 2 * ys)

    def dev(zz, yy, cc):
        return (zz * ys + yy) * 2 + cc

    z_at = [lax.rem(z + step, zs) for step in range(zs)]
    z_peers = [dev(z_at[step], y, core) for step in range(1, zs)]
    y_peer = dev(z, 1 - y, core) if ys == 2 else None
    sibling = dev(z, y, 1 - core)
    partners = z_peers + ([y_peer] if ys == 2 else []) + [sibling]

    reqs, ctx = k_hbm.shape[0], k_hbm.shape[1]
    copies = {}

    def fetch(name, src, dst):
        copies[name] = pltpu.make_async_copy(src, dst, local_sem.at[len(copies)])
        copies[name].start()

    fetch("q", q_hbm, q_buf)
    for p in range(PAIRS):
        cols = pl.ds(p * 2 * HEAD_DIM, 2 * HEAD_DIM)
        fetch(("k", p), k_hbm.at[:, :, cols], k_buf.at[p])
        fetch(("v", p), v_hbm.at[:, :, cols], v_buf.at[p])
    fetch("basis", basis_hbm, basis_buf)
    fetch("coef", coef_hbm, coef_buf)
    fetch("w", w_hbm, w_buf)
    fetch("sob", sob_hbm, sob_buf)

    barrier = pltpu.get_barrier_semaphore()
    for partner in partners:
        pl.semaphore_signal(
            barrier, inc=1, device_id={"adapter": partner}, device_id_type=pl.DeviceIdType.MESH
        )

    payloads = [att_all.at[j] for j in range(KV_HEADS)] + [proj_all, res_all]
    sends = [[] for _ in payloads]

    def send(c, origin, target):
        ref = payloads[c].at[origin]
        copy = pltpu.make_async_remote_copy(
            src_ref=ref,
            dst_ref=ref,
            send_sem=send_sem.at[c, len(sends[c])],
            recv_sem=recv_sem.at[c, origin],
            device_id={"adapter": target},
            device_id_type=pl.DeviceIdType.MESH,
        )
        copy.start()
        sends[c].append(copy)

    def arrive(c, origin):
        ref = payloads[c].at[origin]
        pltpu.make_async_copy(ref, ref, recv_sem.at[c, origin]).wait()

    def stage_own(c):
        for peer in z_peers:
            send(c, me, peer)
        if ys == 2:
            send(c, me, y_peer)
        send(c, me, sibling)

    def stage_z(c):
        for step in range(1, zs):
            origin = dev(z_at[step], y, core)
            arrive(c, origin)
            if ys == 2:
                send(c, origin, y_peer)
            send(c, origin, sibling)

    def stage_y(c):
        if ys == 2:
            for step in range(zs):
                origin = dev(z_at[step], 1 - y, core)
                arrive(c, origin)
                send(c, origin, sibling)

    def stage_core(c):
        for step in range(zs):
            arrive(c, dev(z_at[step], y, 1 - core))
        if ys == 2:
            for step in range(zs):
                arrive(c, dev(z_at[step], 1 - y, 1 - core))

    zero = jnp.zeros((reqs, GROUP, HEAD_DIM), F32)
    copies["q"].wait()
    for p in range(PAIRS):
        q32[p, :, :GROUP, HEAD_DIM:] = zero
        q32[p, :, GROUP:, :HEAD_DIM] = zero
        for h in range(2 * GROUP):
            g = p * 2 * GROUP + h
            lo = (h // GROUP) * HEAD_DIM
            q32[p, :, h, lo : lo + HEAD_DIM] = q_buf[:, g * HEAD_DIM : (g + 1) * HEAD_DIM].astype(F32)
    used = jnp.stack(
        [jnp.full((2 * GROUP, ctx), lengths[r], jnp.int32) for r in range(reqs)]
    )
    valid = lax.broadcasted_iota(jnp.int32, (reqs, 2 * GROUP, ctx), 2) < used

    def attend(p):
        copies[("k", p)].wait()
        scores = jnp.einsum(
            "rhd,rtd->rht", q32[p].astype(BF16), k_buf[p], preferred_element_type=F32
        ) * HEAD_DIM ** (-0.5)
        scores = jnp.where(valid, scores, -1e30)
        row_max = jnp.max(scores, axis=-1, keepdims=True)
        terms = jnp.where(valid, jnp.exp(scores - row_max), 0.0)
        probs = (terms / jnp.sum(terms, axis=-1, keepdims=True)).astype(BF16)
        copies[("v", p)].wait()
        att = jnp.einsum("rht,rtd->rhd", probs, v_buf[p], preferred_element_type=F32)
        a32[p, :, :GROUP, :] = att[:, :GROUP, :HEAD_DIM]
        a32[p, :, GROUP:, :] = att[:, GROUP:, HEAD_DIM:]
        for h in range(2 * GROUP):
            lo = (h % GROUP) * HEAD_DIM
            att_all[2 * p + h // GROUP, me, :, lo : lo + HEAD_DIM] = a32[p, :, h, :].astype(BF16)

    attend(0)
    pl.semaphore_wait(barrier, len(partners))
    stage_own(0)
    stage_own(1)
    attend(1)

    copies["basis"].wait()
    wide = GROUP * HEAD_DIM
    projected = jnp.zeros((reqs, basis_buf.shape[1]), F32)
    for j in range(KV_HEADS):
        projected += jnp.dot(
            att_all[j, me], basis_buf[j * wide : (j + 1) * wide, :], preferred_element_type=F32
        )
    rank = basis_buf.shape[1]
    per_owner = coef_buf.shape[0]
    row_id = lax.broadcasted_iota(jnp.int32, (reqs, HEAD_DIM), 0)
    left = lax.broadcasted_iota(jnp.int32, (reqs, HEAD_DIM), 1) < HEAD_DIM // 2
    id_cols = jnp.zeros((reqs, HEAD_DIM), jnp.int32)
    for r in range(reqs):
        block = lax.div(ids[r], per_owner)
        both = jnp.where(left, block, ids[r] - block * per_owner)
        id_cols = jnp.where(row_id == r, both, id_cols)
    proj_all[me, :, :rank] = projected.astype(BF16)
    proj_all[me, :, rank:] = id_cols.astype(F32).astype(BF16)
    PROJ, RES = KV_HEADS, KV_HEADS + 1
    stage_own(PROJ)
    stage_own(2)
    stage_own(3)

    stage_z(0)
    stage_z(1)
    stage_z(PROJ)
    stage_y(0)
    stage_y(1)
    stage_y(PROJ)
    stage_core(PROJ)

    total = n * reqs
    rows = proj_all[:, :, :rank].reshape(total, rank)
    id_all = proj_all[:, :, rank:].reshape(total, HEAD_DIM)
    half = HEAD_DIM // 2
    owner_col = id_all.astype(F32)[:, :1]
    take = (lax.broadcasted_iota(jnp.int32, (16, HEAD_DIM), 1) == 0).astype(F32).astype(BF16)
    owner_row = lax.dot_general(
        take, id_all, (((1,), (1,)), ((), ())), preferred_element_type=F32
    )[:1, :]
    same = owner_col == owner_row
    r_row = lax.broadcasted_iota(jnp.int32, (total, total), 0)
    r_col = lax.broadcasted_iota(jnp.int32, (total, total), 1)
    slot_row = jnp.sum(jnp.where(same & (r_row < r_col), 1.0, 0.0), axis=0, keepdims=True)
    slot_col = jnp.sum(jnp.where(same & (r_col < r_row), 1.0, 0.0), axis=1, keepdims=True)

    slot_list = lax.broadcasted_iota(jnp.int32, (CAP, total), 0).astype(F32)
    picks = jnp.where(
        (owner_row == me.astype(F32)) & (slot_row == slot_list), 1.0, 0.0
    ).astype(BF16)
    bucket = jnp.dot(picks, rows, preferred_element_type=F32)
    local = jnp.dot(picks, id_all, preferred_element_type=F32)[:, half : half + 1]
    copies["coef"].wait()
    spread = jnp.concatenate(
        [jnp.where(local == float(a), bucket, 0.0).astype(BF16) for a in range(per_owner)], axis=1
    )
    result = jnp.dot(
        spread, coef_buf[...].reshape(per_owner * rank, rank), preferred_element_type=F32
    )
    res_all[me] = result.astype(BF16)
    stage_own(RES)

    copies["w"].wait()

    def base(j):
        return jnp.dot(
            att_all[j].reshape(total, wide),
            w_buf[j * wide : (j + 1) * wide, :],
            preferred_element_type=F32,
        )

    stage_z(2)
    stage_z(3)
    stage_z(RES)
    stage_core(0)
    acc[...] = base(0)
    stage_y(2)
    stage_y(3)
    stage_y(RES)
    stage_core(1)
    acc[...] += base(1)
    stage_core(2)
    acc[...] += base(2)
    stage_core(RES)
    place = jnp.where(
        lax.broadcasted_iota(jnp.int32, (total, n * CAP), 1).astype(F32)
        == owner_col * CAP + slot_col,
        1.0,
        0.0,
    ).astype(BF16)
    adapted = jnp.dot(
        place, res_all[...].reshape(n * CAP, rank), preferred_element_type=F32
    ).astype(BF16)
    copies["sob"].wait()
    acc[...] += lax.dot_general(
        adapted, sob_buf[...], (((1,), (1,)), ((), ())), preferred_element_type=F32
    )
    stage_core(3)
    out_ref[...] = (acc[...] + base(3)).astype(out_ref.dtype)

    for c in range(len(payloads)):
        for copy in sends[c]:
            copy.wait_send()


def on_device(zs, ys, queries, key_cache, value_cache, lengths, ids, w, basis, sob, coef):
    n = zs * ys * 2
    reqs, ctx = key_cache.shape[:2]
    rank = basis.shape[1]
    wide = GROUP * HEAD_DIM
    smem = pl.BlockSpec(memory_space=pltpu.SMEM)
    hbm = pl.BlockSpec(memory_space=pl.ANY)
    vmem = pl.BlockSpec(memory_space=pltpu.VMEM)
    fetches = 5 + 2 * PAIRS
    return pl.pallas_call(
        functools.partial(kernel, zs, ys),
        out_shape=jax.ShapeDtypeStruct((n * reqs, w.shape[1]), BF16),
        in_specs=[smem, smem] + [hbm] * 7,
        out_specs=vmem,
        scratch_shapes=[
            pltpu.VMEM(queries.shape, BF16),
            pltpu.VMEM((PAIRS, reqs, ctx, 2 * HEAD_DIM), BF16),
            pltpu.VMEM((PAIRS, reqs, ctx, 2 * HEAD_DIM), BF16),
            pltpu.VMEM(w.shape, BF16),
            pltpu.VMEM(basis.shape, BF16),
            pltpu.VMEM(sob.shape, BF16),
            pltpu.VMEM(coef.shape, BF16),
            pltpu.VMEM((PAIRS, reqs, 2 * GROUP, 2 * HEAD_DIM), F32),
            pltpu.VMEM((PAIRS, reqs, 2 * GROUP, HEAD_DIM), F32),
            pltpu.VMEM((KV_HEADS, n, reqs, wide), BF16),
            pltpu.VMEM((n, reqs, rank + HEAD_DIM), BF16),
            pltpu.VMEM((n, CAP, rank), BF16),
            pltpu.VMEM((n * reqs, w.shape[1]), F32),
            pltpu.SemaphoreType.DMA((fetches,)),
            pltpu.SemaphoreType.DMA((KV_HEADS + 2, n)),
            pltpu.SemaphoreType.DMA((KV_HEADS + 2, n)),
        ],
        compiler_params=pltpu.CompilerParams(
            collective_id=0, has_side_effects=True, vmem_limit_bytes=58 * 1024 * 1024
        ),
    )(lengths, ids, queries, key_cache, value_cache, w, basis, sob, coef)


def solution(mesh):
    n = mesh.shape["adapter"]
    zs, ys = (4, 2) if n == 16 else (n // 2, 1)
    return jax.shard_map(
        functools.partial(on_device, zs, ys),
        mesh=mesh,
        in_specs=(
            P(("groups", "adapter"), None),
            P(("groups", "adapter"), None, None),
            P(("groups", "adapter"), None, None),
            P(("groups", "adapter")),
            P(("groups", "adapter")),
            P(None, "adapter"),
            P(),
            P("adapter", None),
            P("adapter", None, None),
        ),
        out_specs=P("groups", "adapter"),
        check_vma=False,
    )
```

time: 132 us -> 36.8 us (0.28)
  blocking collectives: 93.2 us -> 0 us
  Pallas kernels: 0 us -> 35 us
  matrix products: 14.5 us -> 0 us
  between operations: 14.2 us -> 0.01 us
  local copies, waits for them, and re-layouts: 7.84 us -> 1.67 us
  other arithmetic: 1.61 us -> 0 us
    psum x1 -> x0, blocking collectives: 61 us -> none  [on_device(): adapter_applied = lax.psum(placed, 'adapter').astype(jnp.bfloat16)]
    pallas_call x0 -> x1, Pallas kernels: none -> 35 us  [on_device(): pl.pallas_call(functools.partial(kernel, zs, ys), out_shape=jax.ShapeDtyp...]
    all_gather x1 -> x0, blocking collectives: 18.5 us -> none  [on_device(): lax.all_gather(projected, 'adapter', axis=0, tiled=True)]
    unnamed x1 -> x0, blocking collectives: 13.7 us -> none
    dot_general x7 -> x0, matrix products: 12.9 us -> none  [the longest x1 4.09 us: on_device(): jnp.dot(lax.all_gather(attended, 'adapter', axis=0, tiled=True), output_w...]
    gather x1 -> x0, local copies, waits for them, and re-layouts: 4.93 us -> none  [on_device(): chosen_coef = coefficients[local_ids]]
    sub x1 -> x0, matrix products: 1.64 us -> none  [attend(): exp_terms = jnp.where(valid_mask, jnp.exp(scores - row_max), 0.0)]
    unnamed x13 -> x1, local copies, waits for them, and re-layouts: 2.72 us -> 1.67 us
  transfers between devices with their start and end apart: 1 -> 0, of which waited for: 0 -> 0; matrix products, arithmetic and copies ran while one was open for 9% -> 0% of each run, Pallas kernels for 0% -> 0%
where the time goes in v1:
time: 36.8 us; the launch traced here: 36.6 us
  Pallas kernels  35 us (95%)
  local copies, waits for them, and re-layouts  1.67 us (5%)
    pallas_call x1, Pallas kernels, on_device(): pl.pallas_call(functools.partial(kernel, zs, ys), out_shape=jax.ShapeDtyp...  35 us
    unnamed x1, local copies, waits for them, and re-layouts  1.67 us

profile of v1, /device:TPU:0, one launch (start us, length us, event | category | flops | bytes accessed | tf_op | source)
XLA Modules:
  0.0 36.6 jit_solution(10843418189465135788)
XLA Ops:
  0.0 35.0 %shard_map.91 = bf16[256,512]{1,0:T(8,128)(2,1)} custom-call(s32[16]{0:T(128)} %lengths.1, s32[16]{0:T(128)} %ids.1, bf16[16,4096]{1,0:T(8,128)(2,1)} %q_hbm.1, bf16[16,160,512]{2,1,0:T(8,128)(2,1)} %k_hbm.1, bf16[16,160,512]{2,1,0:T(8,128)(2,1)} %v_hbm.1, bf16[4096,512]{1,0:T(8,128)(2,1)} %w_hbm.1, bf16[4096,256]{1,0:T(8,128)(2,1)} %basis_hbm.1, ...), custom_call_target="tpu_custom_call" | custom-call | tf_op jit(solution)/shard_map/pallas_call | solution.py:288
  35.0 1.7 %copy.11 = bf16[256,512]{1,0:T(8,128)(2,1)} copy(bf16[256,512]{1,0:T(8,128)(2,1)} %shard_map.91) | data formatting | bytes 524288

commit v2 on v1

--- a/solution.py
+++ b/solution.py
@@ -42,6 +42,7 @@
     att_all,
     proj_all,
     res_all,
+    ids_all,
     acc,
     local_sem,
     send_sem,
@@ -85,7 +86,8 @@
             barrier, inc=1, device_id={"adapter": partner}, device_id_type=pl.DeviceIdType.MESH
         )
 
-    payloads = [att_all.at[j] for j in range(KV_HEADS)] + [proj_all, res_all]
+    PROJ, RES, IDS = KV_HEADS, KV_HEADS + 1, KV_HEADS + 2
+    payloads = [att_all.at[j] for j in range(KV_HEADS)] + [proj_all, res_all, ids_all]
     sends = [[] for _ in payloads]
 
     def send(c, origin, target):
@@ -133,6 +135,17 @@
         if ys == 2:
             for step in range(zs):
                 arrive(c, dev(z_at[step], 1 - y, 1 - core))
+
+    rank = basis_buf.shape[1]
+    per_owner = coef_buf.shape[0]
+    row_id = lax.broadcasted_iota(jnp.int32, (reqs, HEAD_DIM), 0)
+    left = lax.broadcasted_iota(jnp.int32, (reqs, HEAD_DIM), 1) < HEAD_DIM // 2
+    id_cols = jnp.zeros((reqs, HEAD_DIM), jnp.int32)
+    for r in range(reqs):
+        block = lax.div(ids[r], per_owner)
+        both = jnp.where(left, block, ids[r] - block * per_owner)
+        id_cols = jnp.where(row_id == r, both, id_cols)
+    ids_all[me] = id_cols.astype(F32).astype(BF16)
 
     zero = jnp.zeros((reqs, GROUP, HEAD_DIM), F32)
     copies["q"].wait()
@@ -165,11 +178,14 @@
             lo = (h % GROUP) * HEAD_DIM
             att_all[2 * p + h // GROUP, me, :, lo : lo + HEAD_DIM] = a32[p, :, h, :].astype(BF16)
 
+    pl.semaphore_wait(barrier, len(partners))
+    stage_own(IDS)
     attend(0)
-    pl.semaphore_wait(barrier, len(partners))
     stage_own(0)
     stage_own(1)
+    stage_z(IDS)
     attend(1)
+    stage_y(IDS)
 
     copies["basis"].wait()
     wide = GROUP * HEAD_DIM
@@ -178,33 +194,14 @@
         projected += jnp.dot(
             att_all[j, me], basis_buf[j * wide : (j + 1) * wide, :], preferred_element_type=F32
         )
-    rank = basis_buf.shape[1]
-    per_owner = coef_buf.shape[0]
-    row_id = lax.broadcasted_iota(jnp.int32, (reqs, HEAD_DIM), 0)
-    left = lax.broadcasted_iota(jnp.int32, (reqs, HEAD_DIM), 1) < HEAD_DIM // 2
-    id_cols = jnp.zeros((reqs, HEAD_DIM), jnp.int32)
-    for r in range(reqs):
-        block = lax.div(ids[r], per_owner)
-        both = jnp.where(left, block, ids[r] - block * per_owner)
-        id_cols = jnp.where(row_id == r, both, id_cols)
-    proj_all[me, :, :rank] = projected.astype(BF16)
-    proj_all[me, :, rank:] = id_cols.astype(F32).astype(BF16)
-    PROJ, RES = KV_HEADS, KV_HEADS + 1
+    proj_all[me] = projected.astype(BF16)
     stage_own(PROJ)
     stage_own(2)
     stage_own(3)
-
-    stage_z(0)
-    stage_z(1)
-    stage_z(PROJ)
-    stage_y(0)
-    stage_y(1)
-    stage_y(PROJ)
-    stage_core(PROJ)
+    stage_core(IDS)
 
     total = n * reqs
-    rows = proj_all[:, :, :rank].reshape(total, rank)
-    id_all = proj_all[:, :, rank:].reshape(total, HEAD_DIM)
+    id_all = ids_all[...].reshape(total, HEAD_DIM)
     half = HEAD_DIM // 2
     owner_col = id_all.astype(F32)[:, :1]
     take = (lax.broadcasted_iota(jnp.int32, (16, HEAD_DIM), 1) == 0).astype(F32).astype(BF16)
@@ -221,8 +218,19 @@
     picks = jnp.where(
         (owner_row == me.astype(F32)) & (slot_row == slot_list), 1.0, 0.0
     ).astype(BF16)
-    bucket = jnp.dot(picks, rows, preferred_element_type=F32)
     local = jnp.dot(picks, id_all, preferred_element_type=F32)[:, half : half + 1]
+
+    stage_z(0)
+    stage_z(PROJ)
+    stage_z(1)
+    stage_y(0)
+    stage_y(PROJ)
+    stage_z(2)
+    stage_core(PROJ)
+
+    bucket = jnp.dot(
+        picks, proj_all[...].reshape(total, rank), preferred_element_type=F32
+    )
     copies["coef"].wait()
     spread = jnp.concatenate(
         [jnp.where(local == float(a), bucket, 0.0).astype(BF16) for a in range(per_owner)], axis=1
@@ -232,6 +240,8 @@
     )
     res_all[me] = result.astype(BF16)
     stage_own(RES)
+    stage_z(3)
+    stage_y(1)
 
     copies["w"].wait()
 
@@ -242,18 +252,16 @@
             preferred_element_type=F32,
         )
 
-    stage_z(2)
-    stage_z(3)
-    stage_z(RES)
     stage_core(0)
     acc[...] = base(0)
     stage_y(2)
-    stage_y(3)
-    stage_y(RES)
+    stage_z(RES)
     stage_core(1)
     acc[...] += base(1)
+    stage_y(3)
     stage_core(2)
     acc[...] += base(2)
+    stage_y(RES)
     stage_core(RES)
     place = jnp.where(
         lax.broadcasted_iota(jnp.int32, (total, n * CAP), 1).astype(F32)
@@ -301,12 +309,13 @@
             pltpu.VMEM((PAIRS, reqs, 2 * GROUP, 2 * HEAD_DIM), F32),
             pltpu.VMEM((PAIRS, reqs, 2 * GROUP, HEAD_DIM), F32),
             pltpu.VMEM((KV_HEADS, n, reqs, wide), BF16),
-            pltpu.VMEM((n, reqs, rank + HEAD_DIM), BF16),
+            pltpu.VMEM((n, reqs, rank), BF16),
             pltpu.VMEM((n, CAP, rank), BF16),
+            pltpu.VMEM((n, reqs, HEAD_DIM), BF16),
             pltpu.VMEM((n * reqs, w.shape[1]), F32),
             pltpu.SemaphoreType.DMA((fetches,)),
-            pltpu.SemaphoreType.DMA((KV_HEADS + 2, n)),
-            pltpu.SemaphoreType.DMA((KV_HEADS + 2, n)),
+            pltpu.SemaphoreType.DMA((KV_HEADS + 3, n)),
+            pltpu.SemaphoreType.DMA((KV_HEADS + 3, n)),
         ],
         compiler_params=pltpu.CompilerParams(
             collective_id=0, has_side_effects=True, vmem_limit_bytes=58 * 1024 * 1024

time: 36.8 us -> 35 us (0.951)
  Pallas kernels: 35 us -> 33.1 us
    pallas_call x1, Pallas kernels: 35 us -> 33.1 us  [on_device(): pl.pallas_call(functools.partial(kernel, zs, ys), out_shape=jax.ShapeDtyp...]
where the time goes in v2:
time: 35 us; the launch traced here: 34.8 us
  Pallas kernels  33.1 us (95%)
  local copies, waits for them, and re-layouts  1.67 us (5%)
    pallas_call x1, Pallas kernels, on_device(): pl.pallas_call(functools.partial(kernel, zs, ys), out_shape=jax.ShapeDtyp...  33.1 us
    unnamed x1, local copies, waits for them, and re-layouts  1.67 us

profile of v2, /device:TPU:0, one launch (start us, length us, event | category | flops | bytes accessed | tf_op | source)
XLA Modules:
  0.0 34.8 jit_solution(18213413614004158776)
XLA Ops:
  0.0 33.1 %shard_map.91 = bf16[256,512]{1,0:T(8,128)(2,1)} custom-call(s32[16]{0:T(128)} %lengths.1, s32[16]{0:T(128)} %ids.1, bf16[16,4096]{1,0:T(8,128)(2,1)} %q_hbm.1, bf16[16,160,512]{2,1,0:T(8,128)(2,1)} %k_hbm.1, bf16[16,160,512]{2,1,0:T(8,128)(2,1)} %v_hbm.1, bf16[4096,512]{1,0:T(8,128)(2,1)} %w_hbm.1, bf16[4096,256]{1,0:T(8,128)(2,1)} %basis_hbm.1, ...), custom_call_target="tpu_custom_call" | custom-call | tf_op jit(solution)/shard_map/pallas_call | solution.py:296
  33.1 1.7 %copy.11 = bf16[256,512]{1,0:T(8,128)(2,1)} copy(bf16[256,512]{1,0:T(8,128)(2,1)} %shard_map.91) | data formatting | bytes 524288
